TPU v7x, 256 devices: a whole 4x4x8 slice. The times are simulated.
256 devices in a mesh: vocab: 64 (over z, y, core), rows: 4 (over x).
Axes of the slice: x: 4, y: 4, z: 8, core: 2. Of those that a mesh axis runs over, the one named last changes fastest.
Arguments:
- hidden: bfloat16 [2048, 2880], P('rows'), may hold values from -60 to 60, as said below
- head_weight: bfloat16 [2880, 106496], P(None, ('vocab', 'rows')), may hold values from -0.1118034 to 0.1118034, as said below
- eta_level: float32 [2048], P('rows'), may hold values from 0.0001 to 0.003
Outputs:
- filtered_log: float32 [2048, 106496], P('rows', 'vocab')
- entropy: float32 [2048], P('rows')
Inputs may be any that keep to these rules, and one draw needn't show every extreme that they name: `hidden`: real-valued activations. `head_weight`: real-valued weights.
All inputs are finite; a program needn't handle non-finite values.
Results may differ from a plain program's by a relative error of at most 0.0003.
Values may be sent and summed in bfloat16 or wider, within the bound.
A program may use at most 64 MiB of HBM per device.

v0:
```python
import jax
import jax.numpy as jnp
from jax import lax
from jax.sharding import PartitionSpec as P


def from_everyone(shard, axis):
    peers = lax.axis_size(axis)
    return lax.all_to_all(
        jnp.broadcast_to(shard[None], (peers, *shard.shape)), axis, 0, 0, tiled=True
    )


def all_in_one(shard, axis):
    leaves = jax.tree.leaves(shard)
    sequence = sorted(range(len(leaves)), key=lambda k: -leaves[k].size)
    width = (1, *leaves[sequence[0]].shape)[-1]
    lines = [
        jnp.pad(leaves[k].reshape(-1), (0, -leaves[k].size % width)).reshape(-1, width)
        for k in sequence
    ]
    both, at, found = (from_everyone(jnp.concatenate(lines), axis), 0, {})
    for k, line in zip(sequence, lines):
        piece = both[:, at : at + len(line)].reshape(len(both), -1)
        found[k] = piece[:, : leaves[k].size].reshape(-1, *leaves[k].shape)
        at += len(line)
    numbers = iter(range(len(leaves)))
    return jax.tree.map(lambda _: found[next(numbers)], shard)


def combined_pairwise(pieces, combine):
    while len(jax.tree.leaves(pieces)[0]) > 1:
        pieces = jax.vmap(combine)(
            *(jax.tree.map(lambda part: part[side::2], pieces) for side in (0, 1))
        )
    return jax.tree.map(lambda part: part[0], pieces)


def joined_all(shard, axis, combine):
    pieces = all_in_one(shard, axis)
    return combined_pairwise(pieces, combine)


def over_copies(shard, axis):
    return from_everyone(shard, axis).sum(axis=0)


def combine_parts(first, second):
    first_peak, first_total, first_moment = first
    second_peak, second_total, second_moment = second
    top_peak = jnp.maximum(first_peak, second_peak)
    first_factor = jnp.exp(first_peak - top_peak)
    second_factor = jnp.exp(second_peak - top_peak)
    merged_total = first_total * first_factor + second_total * second_factor
    merged_moment = first_factor * (
        first_moment + (first_peak - top_peak) * first_total
    ) + second_factor * (second_moment + (second_peak - top_peak) * second_total)
    return (top_peak, merged_total, merged_moment)


def shards(hidden, head_weight, eta_level):
    scores = jnp.dot(
        hidden,
        lax.all_gather(head_weight, "rows", axis=1, tiled=True),
        preferred_element_type=jnp.float32,
    )
    local_peak = jnp.max(scores, axis=1)
    shifted = jnp.exp(scores - local_peak[:, None])
    local_total = jnp.sum(shifted, axis=1)
    local_moment = jnp.sum(shifted * (scores - local_peak[:, None]), axis=1)
    row_peak, row_total, moment = joined_all(
        (local_peak, local_total, local_moment), "vocab", combine_parts
    )
    shifted = shifted * jnp.exp(local_peak - row_peak)[:, None]
    entropy = jnp.log(row_total) - moment / row_total
    threshold = jnp.minimum(eta_level, jnp.sqrt(eta_level) * jnp.exp(-entropy))
    row_probs = shifted / row_total[:, None]
    kept_weight = jnp.maximum(row_probs - threshold[:, None], 0.0)
    kept_mass = over_copies(jnp.sum(kept_weight, axis=1), "vocab")
    filtered = jnp.log(kept_weight + 0.001 * threshold[:, None]) - jnp.log(kept_mass)[:, None]
    return (filtered, entropy)


def solution(mesh):
    return jax.shard_map(
        shards,
        mesh=mesh,
        in_specs=(P("rows", None), P(None, ("vocab", "rows")), P("rows")),
        out_specs=(P("rows", "vocab"), P("rows")),
        check_vma=False,
    )
```

profile of v0, /device:TPU:7, one launch (start us, length us, event | category | flops | bytes accessed | tf_op | source)
XLA Modules:
  0.0 186.3 jit_solution(3715837613669904508)
XLA Ops:
  7.2 0.0 copy-start
  7.2 0.0 all-gather.2.cloned.1.call-start
  7.2 0.7 all-gather.2.cloned.1.call-update
  7.9 100.7 %all-gather.2.cloned.1.call-done = bf16[2880,1664]{0,1:T(8,128)(2,1)} async-done(((bf16[2880,416]{0,1:T(8,128)(2,1)}), bf16[2880,1664]{0,1:T(8,128)(2,1)}) %all-gather.2.cloned.1.call-update) | async-done | bytes 9584656 | tf_op jit(solution)/shard_map/all_gather | solution.py:64
  108.6 0.0 copy-done
  108.6 9.8 %fusion.10 = (f32[512]{0:T(512)S(1)}, f32[512,1664]{1,0:T(8,128)S(1)}) fusion(bf16[512,2880]{0,1:T(8,128)(2,1)S(1)} %copy-done, bf16[2880,1664]{0,1:T(8,128)(2,1)} %all-gather.2.cloned.1.call-done), kind=kOutput, calls=%fused_computation.37 | convolution fusion | flops 4908187136 | bytes 15943680 | tf_op jit(solution)/shard_map/dot_general | solution.py:62
  118.4 0.0 copy-start.1
  118.4 1.7 copy-done.1
  120.2 1.0 exponential_reduce_fusion
  121.1 0.0 copy-start.2
  121.2 0.1 broadcast_in_dim.4
  121.3 29.0 %all_to_all.11 = f32[64,3,512]{2,1,0:T(4,128)S(1)} all-to-all(f32[64,3,512]{2,1,0:T(4,128)S(1)} %broadcast_in_dim.4), channel_id=1, replica_groups=mesh['vocab'=64,'rows'=4] {'vocab'}, dimensions={0} | all-to-all | bytes 786432 | tf_op jit(solution)/shard_map/all_to_all | solution.py:9
  150.3 0.3 fusion.9
  150.9 0.7 multiply_add_fusion
  151.6 0.8 slice.153
  152.4 0.8 slice.152
  153.9 0.0 copy-done.2
  153.9 0.6 broadcast_multiply_fusion
  154.5 3.8 %fusion.7 = (f32[512]{0:T(512)S(1)}, f32[512,1664]{1,0:T(8,128)}) fusion(f32[512]{0:T(512)S(1)} %get-tuple-element.5, f32[512]{0:T(512)S(1)} %bitcast.19, f32[512]{0:T(512)S(1)} %subtract_exponential_fusion, f32[512,1664]{1,0:T(8,128)} %copy-done.1, f32[512]{0:T(512)S(1)} %get-tuple-element.24), kind=kLoop, calls=%fused_computation.35 | loop fusion | flops 5111296 | bytes 6825984 | tf_op jit(solution)/shard_map/reduce_sum | solution.py:79
  158.3 0.1 broadcast_in_dim.5
  158.4 16.6 %all_to_all.12 = f32[64,1,512]{2,1,0:T(1,128)S(1)} all-to-all(f32[64,1,512]{2,1,0:T(1,128)S(1)} %broadcast_in_dim.5), channel_id=1, replica_groups=mesh['vocab'=64,'rows'=4] {'vocab'}, dimensions={0} | all-to-all | bytes 262144 | tf_op jit(solution)/shard_map/all_to_all | solution.py:9
  175.0 0.1 reduce_sum.39
  175.2 4.3 %log_subtract_fusion = f32[512,1664]{1,0:T(8,128)} fusion(f32[512,1664]{1,0:T(8,128)} %get-tuple-element.8, f32[512]{0:T(512)S(1)} %log.15, f32[512]{0:T(512)S(1)} %get-tuple-element.4), kind=kLoop, calls=%fused_computation.7 | loop fusion | flops 1703936 | bytes 6819840 | tf_op jit(solution)/shard_map/sub | solution.py:80
  (44 shorter events, 0.9 us)
Async XLA Ops:
  7.2 101.4 %copy-start = (bf16[512,2880]{0,1:T(8,128)(2,1)S(1)}, bf16[512,2880]{0,1:T(8,128)(2,1)}, u32[]{:S(2)}) copy-start(bf16[512,2880]{0,1:T(8,128)(2,1)} %param.3) | copy-start | bytes 8847364
  7.2 101.4 %all-gather.2.cloned.1.call-start = ((), (), s32[]{:S(2)}) async-start(), calls=%async_computation.2 | async-start | bytes 12247040 | tf_op jit(solution)/shard_map/all_gather | solution.py:64
  118.4 1.8 copy-start.1
  121.1 32.8 %copy-start.2 = (f32[512]{0:T(512)S(1)}, f32[512]{0:T(512)}, u32[]{:S(2)}) copy-start(f32[512]{0:T(512)} %param.5) | copy-start | bytes 6148
Sparse Core Ops, SparseCore 0:
  9.8 98.7 all-gather.1
where the time goes:
time: 188 us; the launch traced here: 186 us
  waiting for transfers between devices  101 us (54%)
  blocking collectives  45.7 us (24%)
  between operations  14.2 us (8%)
  other arithmetic  10.7 us (6%)
  matrix products  9.81 us (5%)
  local copies, waits for them, and re-layouts  4.51 us (2%)
    all_gather x1, waiting for transfers between devices, shards(): lax.all_gather(head_weight, 'rows', axis=1, tiled=True)  101 us
    all_to_all x2, blocking collectives, from_everyone(): lax.all_to_all(jnp.broadcast_to(shard[None], (peers, *shard.shape)), axis...  45.7 us
    dot_general x1, matrix products, shards(): jnp.dot(hidden, lax.all_gather(head_weight, 'rows', axis=1, tiled=True),...  9.81 us
    sub x1, other arithmetic, shards(): jnp.log(kept_weight + 0.001 * threshold[:, None])  4.27 us
    reduce_sum x1, other arithmetic, shards(): kept_mass = over_copies(jnp.sum(kept_weight, axis=1), 'vocab')  3.84 us
  transfers between devices with their start and end apart: 1, of which 1 were waited for; matrix products, arithmetic and copies ran while one was open for 0% of the time, Pallas kernels for 0%

commit v1 on v0

v1 whole, which is shorter than its diff:
```python
import functools

import jax
import jax.numpy as jnp
from jax import lax
from jax.experimental import pallas as pl
from jax.experimental.pallas import tpu as pltpu
from jax.sharding import PartitionSpec as P

MESH = pl.DeviceIdType.MESH
F32 = jnp.float32
BF16 = jnp.bfloat16

NX, NY, NZ = 4, 4, 8
D = 2880
ROWS = 512
HALF = 256
PART = 128
COLS = 416
WIDE = 512
OUT = NX * COLS

LOG2E = 1.4426950408889634
LN2 = 0.6931471805599453
GAIN = 10.5
BIAS = 123.0
FLOOR = 23.5
NEG = -1e30


def far_first(n):
    return sorted(range(1, n), key=lambda k: -min(k, n - k))


def kernel(
    hid_hbm, w_hbm, eta_ref,
    log_hbm, lkm_ref, ent_ref,
    hid, wraw, wide, codes, stats, got, gstat, out,
    cols, part, zpart, ypart, kept, zkept, ykept,
    load_sem, send_sem, w_sem, x_sem, z_sem, y_sem, code_sem, stat_sem, round_sem, rsend_sem, out_sem,
):
    v = lax.axis_index("vocab")
    x = lax.axis_index("rows")
    z, y, c = v // 8, (v // 2) % 4, v % 2
    sg = 1 - 2 * c

    def at(z, y, c):
        return (z * NY + y) * 2 + c

    here = at(z, y, c)
    sibling = at(z, y, 1 - c)
    zto = [lax.rem(z + k, NZ) for k in range(NZ)]
    yto = [lax.rem(y + k, NY) for k in range(NY)]
    xto = [lax.rem(x + k, NX) for k in range(NX)]
    z_ahead = lax.rem(z + sg + NZ, NZ)
    z_back = lax.rem(z - sg + NZ, NZ)
    y_ahead = lax.rem(y + sg + NY, NY)
    y_back = lax.rem(y - sg + NY, NY)

    zpeers = [(at(zto[k], y, c), x) for k in far_first(NZ)]
    ypeers = [(at(z, yto[k], c), x) for k in (2,)]
    ypeers += [(at(z, yto[k], 1 - c), x) for k in (2, 1, 3)]
    ypeers += [(at(z, yto[k], c), x) for k in (1, 3)] + [(sibling, x)]
    xpeers = [(d, xto[k]) for k in (2, 1, 3) for d in (here, sibling)]

    own = pltpu.make_async_copy(
        hid_hbm.at[pl.ds(pl.multiple_of(HALF * c, HALF), HALF)], hid.at[0], load_sem.at[0])
    own.start()
    own_w = pltpu.make_async_copy(w_hbm, wraw.at[0], load_sem.at[1])
    own_w.start()

    barrier = pltpu.get_barrier_semaphore()
    peers = zpeers + ypeers + xpeers
    for peer in peers:
        pl.semaphore_signal(barrier, 1, device_id=peer, device_id_type=MESH)
    pl.semaphore_wait(barrier, len(peers))

    def y_rows(j):
        return pl.ds(pl.multiple_of(32 * j, 32), 32)

    def z_rows(j):
        return pl.ds(pl.multiple_of(PART + 16 * j, 16), 16)

    def x_send(s, g):
        if g:
            at_row, n = HALF * c + PART + 16 * z, 16
            to = hid.at[NX - s, z_rows(z)]
        else:
            at_row, n = HALF * c + 32 * y, 32
            to = hid.at[NX - s, y_rows(y)]
        pltpu.make_async_remote_copy(
            hid_hbm.at[pl.ds(pl.multiple_of(at_row, 16), n)], to,
            send_sem.at[0], x_sem.at[NX - s, g], device_id=(here, xto[s]), device_id_type=MESH,
        ).start()

    x_send(1, 1)
    x_send(3, 1)
    w_out = pltpu.make_async_remote_copy(
        w_hbm, wraw.at[1], send_sem.at[1], w_sem.at[0], device_id=(sibling, x), device_id_type=MESH)
    w_out.start()
    x_send(1, 0)
    x_send(3, 0)
    x_send(2, 1)
    x_send(2, 0)

    def await_rows(ref, sem):
        pltpu.make_async_copy(ref, ref, sem).wait()

    def z_send(s, j, step, ahead):
        ref = hid.at[s, z_rows(j)]
        pltpu.make_async_remote_copy(
            ref, ref, send_sem.at[0], z_sem.at[s, step, 0 if ahead else 1],
            device_id=(at(z_ahead if ahead else z_back, y, c), x), device_id_type=MESH,
        ).start()

    def y_send(s, j, step, ahead):
        ref = hid.at[s, y_rows(j)]
        pltpu.make_async_remote_copy(
            ref, ref, send_sem.at[0], y_sem.at[s, step, 0 if ahead else 1],
            device_id=(at(z, y_ahead if ahead else y_back, c), x), device_id_type=MESH,
        ).start()

    def z_step(s, t):
        if t == 0:
            await_rows(hid.at[s, z_rows(z)], x_sem.at[s, 1])
            z_send(s, z, 1, True)
            z_send(s, z, 1, False)
            return
        j = lax.rem(z - t * sg + NZ, NZ)
        await_rows(hid.at[s, z_rows(j)], z_sem.at[s, t, 0])
        if t < 4:
            z_send(s, j, t + 1, True)
            j = lax.rem(z + t * sg + NZ, NZ)
            await_rows(hid.at[s, z_rows(j)], z_sem.at[s, t, 1])
            if t < 3:
                z_send(s, j, t + 1, False)

    def y_step(s, t):
        if t == 0:
            await_rows(hid.at[s, y_rows(y)], x_sem.at[s, 0])
            y_send(s, y, 1, True)
            y_send(s, y, 1, False)
            return
        j = lax.rem(y - t * sg + NY, NY)
        await_rows(hid.at[s, y_rows(j)], y_sem.at[s, t, 0])
        if t < 2:
            y_send(s, j, t + 1, True)
            j = lax.rem(y + t * sg + NY, NY)
            await_rows(hid.at[s, y_rows(j)], y_sem.at[s, t, 1])

    rows_of = lax.broadcasted_iota(jnp.int32, (COLS, WIDE), 0)
    lanes_of = lax.broadcasted_iota(jnp.int32, (COLS, WIDE), 1)
    move = jnp.where(lanes_of == rows_of + 32 * x, 1.0, 0.0).astype(BF16)

    def spread(k):
        def body(i, _):
            rows = pl.ds(pl.multiple_of(i * 320, 320), 320)
            wide[rows, WIDE * k : WIDE * (k + 1)] = jnp.dot(
                wraw[k, rows, :], move, preferred_element_type=F32).astype(BF16)
            return 0
        lax.fori_loop(0, D // 320, body, 0)

    own_w.wait()
    cols[...] = jnp.zeros_like(cols)
    part[...] = jnp.zeros_like(part)
    kept[...] = jnp.zeros_like(kept)
    spread(0)
    z_step(1, 0)
    z_step(3, 0)
    y_step(1, 0)
    y_step(3, 0)
    w_out.wait_recv()
    spread(1)
    own.wait()

    plan = [
        [(z_step, 1, 1), (z_step, 3, 1), (z_step, 2, 0)],
        [(y_step, 2, 0), (z_step, 1, 2), (y_step, 1, 1), (y_step, 3, 1)],
        [(z_step, 3, 2), (z_step, 2, 1), (z_step, 1, 3), (y_step, 1, 2)],
        [(z_step, 3, 3), (z_step, 2, 2), (y_step, 2, 1), (z_step, 1, 4)],
        [(z_step, 2, 3), (y_step, 3, 2)],
        [(z_step, 3, 4)],
        [(y_step, 2, 2)],
        [(z_step, 2, 4)],
    ]
    lane = lax.broadcasted_iota(jnp.int32, (PART, WIDE), 1)
    valid = (lane >= 32 * x) & (lane < 32 * x + COLS)
    lane128 = lax.broadcasted_iota(jnp.int32, (PART, 128), 1)

    def chunk(i, _):
        for t, steps in enumerate(plan):
            @pl.when(i == t)
            def _():
                for step, s, n in steps:
                    step(s, n)

        j = i // 2
        g = i % 2
        s = j + jnp.where(j == 2, 1, 0) - jnp.where(j == 3, 1, 0)
        group = 2 * c + g
        block = hid[s, pl.ds(pl.multiple_of(PART * g, PART), PART), :]
        to_x = lax.rem(x + s, NX)
        from_s = lax.rem(NX - s, NX)
        for k in range(2):
            score = jnp.dot(block, wide[:, WIDE * k : WIDE * (k + 1)], preferred_element_type=F32)
            score = jnp.where(valid, score, NEG)
            peak = jnp.max(score, axis=1, keepdims=True)
            t = (score - peak) * LOG2E
            e = jnp.exp2(t)
            total = jnp.sum(e, axis=1, keepdims=True)
            moment = jnp.sum(e * t, axis=1, keepdims=True)
            code = jnp.exp2(jnp.maximum(t, -FLOOR) * GAIN + BIAS).astype(BF16)
            stat = jnp.where(lane128 == 0, peak, jnp.where(lane128 == 1, total, moment))
            stat = stat.T[0:8]
            codes[i, k] = code
            stats[i, k] = stat

            def send():
                pltpu.make_async_remote_copy(
                    codes.at[i, k], got.at[x, pl.ds(pl.multiple_of(PART * group, PART), PART)],
                    send_sem.at[2], code_sem.at[from_s, k, g],
                    device_id=(sibling if k else here, to_x), device_id_type=MESH,
                ).start()
                pltpu.make_async_remote_copy(
                    stats.at[i, k], gstat.at[x, group],
                    send_sem.at[3], stat_sem.at[from_s, k, g],
                    device_id=(sibling if k else here, to_x), device_id_type=MESH,
                ).start()

            if k == 0:
                @pl.when(i < 2)
                def _():
                    got[x, pl.ds(pl.multiple_of(PART * group, PART), PART), :] = code
                    gstat[x, group] = stat
                pl.when(i >= 2)(send)
            else:
                send()
        return 0

    lax.fori_loop(0, 8, chunk, 0)

    def await_group(ref_of, sem):
        for s in range(NX):
            for k in range(2):
                if s == 0 and k == 0:
                    continue
                for g in range(2):
                    ref = ref_of(xto[s], 2 * ((1 - c) if k else c) + g)
                    pltpu.make_async_copy(ref, ref, sem.at[s, k, g]).wait()

    await_group(lambda xs, group: gstat.at[xs, group], stat_sem)

    def combined(peaks, totals, moments):
        top = functools.reduce(jnp.maximum, peaks)
        total = moment = None
        for a, b, d in zip(peaks, totals, moments):
            low = (a - top) * LOG2E
            f = jnp.exp2(low)
            p, q = b * f, f * (d + low * b)
            total = p if total is None else total + p
            moment = q if moment is None else moment + q
        return top, total, moment

    def swap(mine, slots, place, peers, n):
        slots[place] = mine[...]
        for peer in peers:
            pltpu.make_async_remote_copy(
                mine, slots.at[place], rsend_sem.at[n], round_sem.at[n],
                device_id=peer, device_id_type=MESH,
            ).start()
        seven = slots.at[pl.ds(0, 7)]
        pltpu.make_async_copy(seven, seven, round_sem.at[n]).wait()
        pltpu.make_async_copy(seven, seven, rsend_sem.at[n]).wait()

    peaks = [gstat[k, :, 0, :] for k in range(NX)]
    top, total, moment = combined(
        peaks, [gstat[k, :, 1, :] for k in range(NX)], [gstat[k, :, 2, :] for k in range(NX)])
    yc = y * 2 + c
    for slots, place, peer_set, n in ((zpart, z, zpeers, 0), (ypart, yc, ypeers, 1)):
        part[0:4] = top
        part[4:8] = total
        part[8:12] = moment
        swap(part, slots, place, peer_set, n)
        top, total, moment = combined(
            [slots[k, 0:4] for k in range(8)], [slots[k, 4:8] for k in range(8)],
            [slots[k, 8:12] for k in range(8)])

    eta = eta_ref[...]
    entropy = jnp.log(total) - moment / total * LN2
    limit = jnp.minimum(eta, jnp.sqrt(eta) * jnp.exp(-entropy))
    ent_ref[...] = entropy
    under = jnp.log2(total) + BIAS / GAIN
    for k in range(NX):
        cols[:, k, :] = (peaks[k] - top) * LOG2E - under
    cols[:, NX, :] = limit

    await_group(lambda xs, group: got.at[xs, pl.ds(pl.multiple_of(PART * group, PART), PART)], code_sem)

    def finish(group, _):
        rows = pl.ds(pl.multiple_of(PART * group, PART), PART)
        col = cols[group].T
        shift = [col[:, k : k + 1] for k in range(NX)]
        cut = col[:, NX : NX + 1]
        least = 0.001 * cut
        acc = jnp.zeros((PART, 128), F32)
        for tile in range(OUT // 128):
            k = min(tile // 3, NX - 1)
            sent = got[k, rows, 128 * (tile - 3 * k) : 128 * (tile - 3 * k) + 128].astype(F32)
            off = shift[k]
            if tile % 3 == 0 and 0 < tile < 12:
                left = got[k - 1, rows, 384:512].astype(F32)
                sent = jnp.where(lane128 < 32 * k, left, sent)
                off = jnp.where(lane128 < 32 * k, shift[k - 1], shift[k])
            prob = jnp.exp2(jnp.log2(sent) * (1.0 / GAIN) + off)
            keep = jnp.maximum(prob - cut, 0.0)
            acc = acc + keep
            out[rows, 128 * tile : 128 * tile + 128] = jnp.log(keep + least)
        kept[pl.ds(group, 1)] = jnp.sum(acc.T, axis=0, keepdims=True)
        pltpu.make_async_copy(out.at[rows], log_hbm.at[rows], out_sem.at[group]).start()
        return 0

    lax.fori_loop(0, 4, finish, 0)

    for slots, place, peer_set, n in ((zkept, z, zpeers, 2), (ykept, yc, ypeers, 3)):
        swap(kept, slots, place, peer_set, n)
        mass = slots[0]
        for k in range(1, 8):
            mass = mass + slots[k]
        kept[...] = mass
    lkm_ref[...] = jnp.log(kept[0:4])

    for n, ref in ((0, hid.at[pl.ds(0, 3)]), (2, codes.at[pl.ds(0, 7)]), (3, stats.at[pl.ds(0, 7)])):
        pltpu.make_async_copy(ref, ref, send_sem.at[n]).wait()
    w_out.wait_send()
    for group in range(4):
        rows = pl.ds(PART * group, PART)
        pltpu.make_async_copy(out.at[rows], log_hbm.at[rows], out_sem.at[group]).wait()


def shards(hidden, head_weight, eta_level):
    dma = pltpu.SemaphoreType.DMA
    vmem = pltpu.VMEM
    logs, lkm, ent = pl.pallas_call(
        kernel,
        out_shape=(
            jax.ShapeDtypeStruct((ROWS, OUT), F32),
            jax.ShapeDtypeStruct((4, 128), F32),
            jax.ShapeDtypeStruct((4, 128), F32),
        ),
        in_specs=[
            pl.BlockSpec(memory_space=pl.ANY),
            pl.BlockSpec(memory_space=pl.ANY),
            pl.BlockSpec(memory_space=vmem),
        ],
        out_specs=(
            pl.BlockSpec(memory_space=pl.ANY),
            pl.BlockSpec(memory_space=vmem),
            pl.BlockSpec(memory_space=vmem),
        ),
        scratch_shapes=[
            vmem((NX, HALF, D), BF16),
            vmem((2, D, COLS), BF16),
            vmem((D, 2 * WIDE), BF16),
            vmem((8, 2, PART, WIDE), BF16),
            vmem((8, 2, 8, 128), F32),
            vmem((NX, ROWS, WIDE), BF16),
            vmem((NX, 4, 8, 128), F32),
            vmem((ROWS, OUT), F32),
            vmem((4, 128, 128), F32),
            vmem((16, 128), F32),
            vmem((8, 16, 128), F32),
            vmem((8, 16, 128), F32),
            vmem((8, 128), F32),
            vmem((8, 8, 128), F32),
            vmem((8, 8, 128), F32),
            dma((2,)),
            dma((4,)),
            dma((1,)),
            dma((NX, 2)),
            dma((NX, 5, 2)),
            dma((NX, 3, 2)),
            dma((NX, 2, 2)),
            dma((NX, 2, 2)),
            dma((4,)),
            dma((4,)),
            dma((4,)),
        ],
        compiler_params=pltpu.CompilerParams(
            collective_id=0, has_side_effects=True, vmem_limit_bytes=56 * 2**20),
        cost_estimate=pl.CostEstimate(
            flops=2 * ROWS * D * OUT, bytes_accessed=10 * 2**20, transcendentals=5 * ROWS * OUT),
        name="eta_filter",
    )(hidden, head_weight, eta_level.reshape(4, 128))
    return logs - lkm.reshape(ROWS)[:, None], ent.reshape(ROWS)


def solution(mesh):
    return jax.shard_map(
        shards,
        mesh=mesh,
        in_specs=(P("rows", None), P(None, ("vocab", "rows")), P("rows")),
        out_specs=(P("rows", "vocab"), P("rows")),
        check_vma=False,
    )
```

time: 188 us -> 98.3 us (0.52)
  waiting for transfers between devices: 101 us -> 0 us
  Pallas kernels: 0 us -> 85.4 us
  blocking collectives: 45.7 us -> 0 us
  between operations: 14.2 us -> 0.66 us
  matrix products: 9.81 us -> 0 us
  other arithmetic: 10.7 us -> 4 us
  local copies, waits for them, and re-layouts: 4.51 us -> 8.15 us
    all_gather x1 -> x0, waiting for transfers between devices: 101 us -> none  [shards(): lax.all_gather(head_weight, 'rows', axis=1, tiled=True)]
    pallas_call x0 -> x1, Pallas kernels: none -> 85.4 us  [shards(): pl.pallas_call(kernel, out_shape=(jax.ShapeDtypeStruct((ROWS, OUT), F32),...]
    all_to_all x2 -> x0, blocking collectives: 45.7 us -> none  [from_everyone(): lax.all_to_all(jnp.broadcast_to(shard[None], (peers, *shard.shape)), axis...]
    dot_general x1 -> x0, matrix products: 9.81 us -> none  [shards(): jnp.dot(hidden, lax.all_gather(head_weight, 'rows', axis=1, tiled=True),...]
    unnamed x7, local copies, waits for them, and re-layouts: 1.77 us -> 8.15 us
    reduce_sum x3 -> x0, other arithmetic: 4.93 us -> none  [the longest x1 3.84 us: shards(): kept_mass = over_copies(jnp.sum(kept_weight, axis=1), 'vocab')]
    slice x31 -> x0, local copies, waits for them, and re-layouts: 2.57 us -> none  [the longest x30 2.3 us: combined_pairwise(): part[side::2]]
  transfers between devices with their start and end apart: 1 -> 0, of which waited for: 1 -> 0; matrix products, arithmetic and copies ran while one was open for 0% -> 0% of each run, Pallas kernels for 0% -> 0%
where the time goes in v1:
time: 98.3 us; the launch traced here: 98.2 us
  Pallas kernels  85.4 us (87%)
  local copies, waits for them, and re-layouts  8.15 us (8%)
  other arithmetic  4 us (4%)
    pallas_call x1, Pallas kernels, shards(): pl.pallas_call(kernel, out_shape=(jax.ShapeDtypeStruct((ROWS, OUT), F32),...  85.4 us
    unnamed x7, local copies, waits for them, and re-layouts  8.15 us
    sub x1, other arithmetic, shards(): return (logs - lkm.reshape(ROWS)[:, None], ent.reshape(ROWS))  4 us

profile of v1, /device:TPU:7, one launch (start us, length us, event | category | flops | bytes accessed | tf_op | source)
XLA Modules:
  0.0 98.2 jit_solution(2906313895165714735)
XLA Ops:
  0.6 0.0 copy-start
  0.6 4.6 %copy.6.w_hbm = bf16[2880,416]{1,0:T(8,128)(2,1)} copy(bf16[2880,416]{0,1:T(8,128)(2,1)} %param.4) | data formatting | bytes 4792320 | tf_op args[1]
  5.2 0.0 copy-done
  5.2 3.0 %copy.5.hid_hbm = bf16[512,2880]{1,0:T(8,128)(2,1)} copy(bf16[512,2880]{0,1:T(8,128)(2,1)S(1)} %copy-done) | data formatting | bytes 5898240 | tf_op args[0]
  8.2 85.4 %eta_filter.1 = (f32[512,1664]{1,0:T(8,128)}, f32[4,128]{1,0:T(4,128)}, f32[4,128]{1,0:T(4,128)}) custom-call(bf16[512,2880]{1,0:T(8,128)(2,1)} %copy.5.hid_hbm, bf16[2880,416]{1,0:T(8,128)(2,1)} %copy.6.w_hbm, f32[4,128]{1,0:T(4,128)} %bitcast.5), custom_call_target="tpu_custom_call" | custom-call | flops 4907335680 | bytes 10485760 | tf_op jit(solution)/shard_map/eta_filter/pallas_call | solution.py:343
  93.6 0.0 copy-start.1
  93.6 4.0 %broadcast_subtract_fusion = f32[512,1664]{1,0:T(8,128)} fusion(f32[512,1664]{1,0:T(8,128)} %get-tuple-element.5, f32[512]{0:T(512)} %bitcast.3), kind=kLoop, calls=%fused_computation | loop fusion | flops 851968 | bytes 6817792 | tf_op jit(solution)/shard_map/sub | solution.py:394
  97.6 0.0 copy-done.1
  97.6 0.6 copy.8
Async XLA Ops:
  0.6 4.6 %copy-start = (bf16[512,2880]{0,1:T(8,128)(2,1)S(1)}, bf16[512,2880]{0,1:T(8,128)(2,1)}, u32[]{:S(2)}) copy-start(bf16[512,2880]{0,1:T(8,128)(2,1)} %param.3) | copy-start | bytes 8847364
  93.6 4.0 %copy-start.1 = (f32[4,128]{1,0:T(4,128)S(1)}, f32[4,128]{1,0:T(4,128)}, u32[]{:S(2)}) copy-start(f32[4,128]{1,0:T(4,128)} %get-tuple-element.7) | copy-start | bytes 6148

commit v2 on v1

v2 whole, which is shorter than its diff:
```python
import functools

import jax
import jax.numpy as jnp
from jax import lax
from jax.experimental import pallas as pl
from jax.experimental.pallas import tpu as pltpu
from jax.sharding import PartitionSpec as P

MESH = pl.DeviceIdType.MESH
F32 = jnp.float32
BF16 = jnp.bfloat16

NX, NY, NZ = 4, 4, 8
D = 2880
ROWS = 512
COLS = 416
OUT = NX * COLS
YPART = 432
ZPART = 144

LOG2E = 1.4426950408889634
LN2 = 0.6931471805599453
GAIN = 10.5
BIAS = 123.0
FLOOR = 23.5


def far_first(n):
    return sorted(range(1, n), key=lambda k: -min(k, n - k))


PLACE = {(1, 0): (1, 0), (3, 0): (1, 1), (1, 1): (2, 0), (3, 1): (2, 1), (2, 0): (3, 0), (2, 1): (3, 1)}


def kernel(
    hid_hbm, w_hbm, eta_ref,
    log_ref, lkm_ref, ent_ref,
    hid, w, codes, stats, got, gstat, keep,
    cols, part, zpart, ypart, kept, zkept, ykept,
    load_sem, send_sem, w_sem, x_sem, z_sem, y_sem, code_sem, stat_sem, round_sem, rsend_sem,
):
    v = lax.axis_index("vocab")
    x = lax.axis_index("rows")
    z, y, c = v // 8, (v // 2) % 4, v % 2
    sg = 1 - 2 * c

    def at(z, y, c):
        return (z * NY + y) * 2 + c

    here = at(z, y, c)
    sibling = at(z, y, 1 - c)
    zto = [lax.rem(z + k, NZ) for k in range(NZ)]
    yto = [lax.rem(y + k, NY) for k in range(NY)]
    xto = [lax.rem(x + k, NX) for k in range(NX)]
    x_ahead, x_back = lax.rem(x + sg + NX, NX), lax.rem(x - sg + NX, NX)
    y_ahead, y_back = lax.rem(y + sg + NY, NY), lax.rem(y - sg + NY, NY)
    z_ahead, z_back = lax.rem(z + sg + NZ, NZ), lax.rem(z - sg + NZ, NZ)

    zpeers = [(at(zto[k], y, c), x) for k in far_first(NZ)]
    ypeers = [(at(z, yto[2], c), x)]
    ypeers += [(at(z, yto[k], 1 - c), x) for k in (2, 1, 3)]
    ypeers += [(at(z, yto[k], c), x) for k in (1, 3)] + [(sibling, x)]
    xpeers = [(d, xto[k]) for k in (2, 1, 3) for d in (here, sibling)]

    barrier = pltpu.get_barrier_semaphore()
    peers = zpeers + ypeers + xpeers
    for peer in peers:
        pl.semaphore_signal(barrier, 1, device_id=peer, device_id_type=MESH)

    def lanes_of(lg):
        return pl.ds(pl.multiple_of(256 * c + 128 * lg, 128), 128)

    own = [
        pltpu.make_async_copy(hid_hbm.at[:, lanes_of(lg)], hid.at[0, lg], load_sem.at[lg])
        for lg in range(2)
    ]
    own.append(pltpu.make_async_copy(w_hbm, w.at[0], load_sem.at[2]))
    for copy in own:
        copy.start()
    part[...] = jnp.zeros_like(part)
    kept[...] = jnp.zeros_like(kept)
    pl.semaphore_wait(barrier, len(peers))

    def y_rows(j):
        return pl.ds(pl.multiple_of(YPART * j, 16), YPART)

    def z_rows(j):
        return pl.ds(pl.multiple_of(NY * YPART + ZPART * j, 16), ZPART)

    def hid_at(role, lg, rows):
        p, q = PLACE[role, lg]
        return hid.at[p, q, rows]

    def x_send(lg, along_z, ahead):
        rows = z_rows(z) if along_z else y_rows(y)
        role = 3 if ahead else 1
        pltpu.make_async_remote_copy(
            hid_hbm.at[rows, lanes_of(lg)], hid_at(role, lg, rows),
            send_sem.at[0], x_sem.at[role, lg, along_z],
            device_id=(here, x_ahead if ahead else x_back), device_id_type=MESH,
        ).start()

    x_send(1, 1, True)
    x_send(0, 1, True)
    x_send(1, 0, False)
    x_send(0, 1, False)
    w_out = pltpu.make_async_remote_copy(
        w_hbm, w.at[1], send_sem.at[1], w_sem.at[0], device_id=(sibling, x), device_id_type=MESH)
    w_out.start()
    x_send(1, 1, False)
    x_send(0, 0, False)
    x_send(0, 0, True)
    x_send(1, 0, True)

    def arrived(ref, sem):
        pltpu.make_async_copy(ref, ref, sem).wait()

    def pass_on(ref, sem, device):
        pltpu.make_async_remote_copy(
            ref, ref, send_sem.at[0], sem, device_id=device, device_id_type=MESH).start()

    def x_step(role, lg, along_z):
        rows = z_rows(z) if along_z else y_rows(y)
        ref = hid_at(role, lg, rows)
        arrived(ref, x_sem.at[role, lg, along_z])
        if role == (1 if along_z else 3):
            pltpu.make_async_remote_copy(
                ref, hid_at(2, lg, rows), send_sem.at[0], x_sem.at[2, lg, along_z],
                device_id=(here, x_back if along_z else x_ahead), device_id_type=MESH,
            ).start()

    def z_begin(role, lg):
        ref = hid_at(role, lg, z_rows(z))
        pass_on(ref, z_sem.at[role, lg, 1, 0], (at(z_ahead, y, c), x))
        pass_on(ref, z_sem.at[role, lg, 1, 1], (at(z_back, y, c), x))

    def z_step(role, lg, t, way):
        side = (1 - way) // 2
        ref = hid_at(role, lg, z_rows(lax.rem(z - way * t * sg + NZ, NZ)))
        arrived(ref, z_sem.at[role, lg, t, side])
        if t < (4, 3)[side]:
            pass_on(ref, z_sem.at[role, lg, t + 1, side], (at((z_ahead, z_back)[side], y, c), x))

    def y_begin(role, lg):
        ref = hid_at(role, lg, y_rows(y))
        pass_on(ref, y_sem.at[role, lg, 1, 0], (at(z, y_ahead, c), x))
        pass_on(ref, y_sem.at[role, lg, 1, 1], (at(z, y_back, c), x))

    def y_step(role, lg, t, way):
        side = (1 - way) // 2
        ref = hid_at(role, lg, y_rows(lax.rem(y - way * t * sg + NY, NY)))
        arrived(ref, y_sem.at[role, lg, t, side])
        if t < (2, 1)[side]:
            pass_on(ref, y_sem.at[role, lg, t + 1, side], (at(z, (y_ahead, y_back)[side], c), x))

    def own_here():
        for copy in own:
            copy.wait()

    plan = [
        [
            (own_here,),
        ],
        [
            (x_step, 3, 1, 1), (z_begin, 3, 1), (x_step, 3, 0, 1), (z_begin, 3, 0), (x_step, 1, 1, 0),
            (y_begin, 1, 1), (x_step, 1, 0, 1), (x_step, 1, 1, 1), (z_begin, 1, 0), (z_step, 3, 1, 1, 1),
            (x_step, 1, 0, 0), (y_begin, 1, 0), (z_step, 3, 0, 1, 1), (z_begin, 1, 1),
            (z_step, 3, 1, 1, -1), (x_step, 3, 0, 0), (y_begin, 3, 0), (z_step, 3, 0, 1, -1),
            (z_step, 1, 0, 1, 1), (x_step, 3, 1, 0), (x_step, 2, 0, 1), (z_begin, 2, 0), (x_step, 2, 1, 1),
            (z_step, 1, 0, 1, -1), (z_begin, 2, 1), (y_begin, 3, 1), (z_step, 3, 1, 2, 1),
            (w_out.wait_recv,), (z_step, 1, 1, 1, 1),
        ],
        [
            (z_step, 3, 0, 2, 1), (z_step, 1, 0, 2, 1), (y_step, 1, 0, 1, 1), (y_step, 1, 1, 1, -1),
            (z_step, 1, 1, 1, -1), (z_step, 3, 0, 2, -1), (x_step, 2, 1, 0), (y_step, 1, 0, 1, -1),
            (z_step, 2, 1, 1, 1), (z_step, 2, 0, 1, 1), (z_step, 3, 1, 2, -1), (x_step, 2, 0, 0),
            (z_step, 1, 1, 2, 1), (y_step, 3, 0, 1, 1), (z_step, 2, 1, 1, -1), (z_step, 1, 0, 2, -1),
            (z_step, 2, 0, 1, -1), (y_begin, 2, 0), (z_step, 3, 1, 3, 1), (z_step, 3, 0, 3, 1),
            (y_step, 1, 1, 1, 1), (z_step, 1, 0, 3, 1), (y_step, 3, 1, 1, -1), (y_step, 3, 0, 1, -1),
            (z_step, 2, 0, 2, 1), (z_step, 3, 1, 3, -1), (z_step, 1, 1, 2, -1), (y_step, 3, 1, 1, 1),
            (y_begin, 2, 1), (z_step, 1, 1, 3, 1), (y_step, 1, 0, 2, 1), (z_step, 1, 0, 3, -1),
            (z_step, 2, 1, 2, -1), (z_step, 3, 0, 3, -1), (z_step, 2, 0, 2, -1), (z_step, 2, 1, 2, 1),
            (y_step, 3, 0, 2, 1), (y_step, 2, 0, 1, 1), (z_step, 3, 0, 4, 1), (z_step, 1, 0, 4, 1),
        ],
        [
            (z_step, 2, 0, 3, 1), (z_step, 1, 1, 3, -1),
        ],
        [
            (y_step, 1, 1, 2, 1), (z_step, 1, 1, 4, 1), (y_step, 3, 1, 2, 1), (z_step, 3, 1, 4, 1),
            (z_step, 2, 1, 3, 1), (y_step, 2, 0, 1, -1), (y_step, 2, 1, 1, 1),
        ],
        [
            (z_step, 2, 0, 3, -1), (z_step, 2, 0, 4, 1),
        ],
        [
            (z_step, 2, 1, 3, -1), (y_step, 2, 0, 2, 1), (y_step, 2, 1, 1, -1), (z_step, 2, 1, 4, 1),
            (y_step, 2, 1, 2, 1),
        ],
        [],
    ]

    def chunk(i, _):
        for t, steps in enumerate(plan):
            @pl.when(i == t)
            def _():
                for step, *rest in steps:
                    step(*rest)

        p, k = i // 2, i % 2
        score = jnp.dot(
            w[k], jnp.concatenate([hid[p, 0], hid[p, 1]], axis=1), preferred_element_type=F32)
        peak = jnp.max(score, axis=0, keepdims=True)
        t = (score - peak) * LOG2E
        e = jnp.exp2(t)
        total = jnp.sum(e, axis=0, keepdims=True)
        moment = jnp.sum(e * t, axis=0, keepdims=True)
        code = jnp.exp2(jnp.maximum(t, -FLOOR) * GAIN + BIAS).astype(BF16)
        for q in range(2):
            lanes = slice(128 * q, 128 * q + 128)
            codes[i, q] = code[:, lanes]
            for n, row in enumerate((peak, total, moment)):
                stats[i, q, n : n + 1] = row[:, lanes]
        cols_here = pl.ds(pl.multiple_of(COLS * x, 16), COLS)

        @pl.when(i == 0)
        def _():
            for q in range(2):
                got[c, q, cols_here] = codes[i, q]
                gstat[x, 2 * c + q] = stats[i, q]

        def send(i, k, piece, land, sems, n):
            for q in range(2):
                role = jnp.where(p == 0, 0, jnp.where(p == 3, 2, 1 + 2 * q))
                lg = jnp.where((p == 0) | (p == 3), q, p - 1)
                device = (at(z, y, jnp.where(k == 1, 1 - c, c)), lax.rem(x + role * sg + NX, NX))
                pltpu.make_async_remote_copy(
                    piece.at[i, q], land(lg), send_sem.at[n], sems.at[x, c, lg],
                    device_id=device, device_id_type=MESH,
                ).start()

        def send_stats(i, k):
            send(i, k, stats, lambda lg: gstat.at[x, 2 * c + lg], stat_sem, 3)

        def send_codes(i, k):
            send(i, k, codes, lambda lg: got.at[c, lg, cols_here], code_sem, 2)

        @pl.when(i > 0)
        def _():
            send_stats(i, k)

        @pl.when((i > 0) & (i < 6))
        def _():
            send_codes(i, k)

        @pl.when(i == 7)
        def _():
            send_codes(6, 0)
            send_codes(7, 1)

        return 0

    lax.fori_loop(0, 8, chunk, 0)

    def await_groups(ref_of, sem):
        for s in range(NX):
            for h in ((1 - c,) if s == 0 else (c, 1 - c)):
                for lg in range(2):
                    ref = ref_of(xto[s], h, lg)
                    pltpu.make_async_copy(ref, ref, sem.at[xto[s], h, lg]).wait()

    await_groups(lambda xs, h, lg: gstat.at[xs, 2 * h + lg], stat_sem)

    def combined(peaks, totals, moments):
        top = functools.reduce(jnp.maximum, peaks)
        total = moment = None
        for a, b, d in zip(peaks, totals, moments):
            low = (a - top) * LOG2E
            f = jnp.exp2(low)
            m, n = b * f, f * (d + low * b)
            total = m if total is None else total + m
            moment = n if moment is None else moment + n
        return top, total, moment

    def swap_start(mine, slots, place, peers, n):
        slots[place] = mine[...]
        for peer in peers:
            pltpu.make_async_remote_copy(
                mine, slots.at[place], rsend_sem.at[n], round_sem.at[n],
                device_id=peer, device_id_type=MESH,
            ).start()

    def swap_end(slots, n):
        seven = slots.at[pl.ds(0, 7)]
        pltpu.make_async_copy(seven, seven, round_sem.at[n]).wait()
        pltpu.make_async_copy(seven, seven, rsend_sem.at[n]).wait()

    peaks = [gstat[k, :, 0, :] for k in range(NX)]
    top, total, moment = combined(
        peaks, [gstat[k, :, 1, :] for k in range(NX)], [gstat[k, :, 2, :] for k in range(NX)])
    yc = y * 2 + c
    for slots, place_at, peer_set, n in ((zpart, z, zpeers, 0), (ypart, yc, ypeers, 1)):
        part[0:4] = top
        part[4:8] = total
        part[8:12] = moment
        swap_start(part, slots, place_at, peer_set, n)
        swap_end(slots, n)
        top, total, moment = combined(
            [slots[k, 0:4] for k in range(8)], [slots[k, 4:8] for k in range(8)],
            [slots[k, 8:12] for k in range(8)])

    eta = eta_ref[...]
    entropy = jnp.log(total) - moment / total * LN2
    limit = jnp.minimum(eta, jnp.sqrt(eta) * jnp.exp(-entropy))
    ent_ref[...] = entropy
    under = jnp.log2(total) + BIAS / GAIN
    for k in range(NX):
        cols[:, k, :] = (peaks[k] - top) * LOG2E - under
    cols[:, NX, :] = limit

    await_groups(lambda xs, h, lg: got.at[h, lg, pl.ds(pl.multiple_of(COLS * xs, 16), COLS)], code_sem)

    def weigh(group, _):
        cut = cols[group, NX : NX + 1]
        mass = jnp.zeros((1, 128), F32)
        for k in range(NX):
            sent = got[group // 2, group % 2, COLS * k : COLS * (k + 1)].astype(F32)
            prob = jnp.exp2(jnp.log2(sent) * (1.0 / GAIN) + cols[group, k : k + 1])
            weight = jnp.maximum(prob - cut, 0.0)
            keep[group, COLS * k : COLS * (k + 1)] = weight
            mass = mass + jnp.sum(weight, axis=0, keepdims=True)
        kept[pl.ds(group, 1)] = mass
        return 0

    lax.fori_loop(0, 4, weigh, 0)

    def finish(group, _):
        least = 0.001 * cols[group, NX : NX + 1]
        rows = pl.ds(pl.multiple_of(128 * group, 128), 128)
        for tile in range(OUT // 128):
            at_tile = slice(128 * tile, 128 * tile + 128)
            log_ref[rows, at_tile] = jnp.log(keep[group, at_tile] + least).T
        return 0

    for slots, place_at, peer_set, n in ((zkept, z, zpeers, 2), (ykept, yc, ypeers, 3)):
        swap_start(kept, slots, place_at, peer_set, n)
        lax.fori_loop(2 * n - 4, 2 * n - 2, finish, 0)
        swap_end(slots, n)
        mass = slots[0]
        for k in range(1, 8):
            mass = mass + slots[k]
        kept[...] = mass
    lkm_ref[...] = jnp.log(kept[0:4])

    for n, ref in ((0, hid.at[pl.ds(0, 3)]), (2, codes.at[pl.ds(0, 7)]), (3, stats.at[pl.ds(0, 7)])):
        pltpu.make_async_copy(ref, ref, send_sem.at[n]).wait()
    w_out.wait_send()


def shards(hidden, head_weight, eta_level):
    dma = pltpu.SemaphoreType.DMA
    vmem = pltpu.VMEM
    logs, lkm, ent = pl.pallas_call(
        kernel,
        out_shape=(
            jax.ShapeDtypeStruct((ROWS, OUT), F32),
            jax.ShapeDtypeStruct((4, 128), F32),
            jax.ShapeDtypeStruct((4, 128), F32),
        ),
        in_specs=[
            pl.BlockSpec(memory_space=pltpu.HBM),
            pl.BlockSpec(memory_space=pltpu.HBM),
            pl.BlockSpec(memory_space=vmem),
        ],
        out_specs=(
            pl.BlockSpec(memory_space=vmem),
            pl.BlockSpec(memory_space=vmem),
            pl.BlockSpec(memory_space=vmem),
        ),
        scratch_shapes=[
            vmem((4, 2, D, 128), BF16),
            vmem((2, COLS, D), BF16),
            vmem((8, 2, COLS, 128), BF16),
            vmem((8, 2, 8, 128), F32),
            vmem((2, 2, OUT, 128), BF16),
            vmem((NX, 4, 8, 128), F32),
            vmem((4, OUT, 128), F32),
            vmem((4, 8, 128), F32),
            vmem((16, 128), F32),
            vmem((8, 16, 128), F32),
            vmem((8, 16, 128), F32),
            vmem((8, 128), F32),
            vmem((8, 8, 128), F32),
            vmem((8, 8, 128), F32),
            dma((3,)),
            dma((4,)),
            dma((1,)),
            dma((4, 2, 2)),
            dma((4, 2, 5, 2)),
            dma((4, 2, 3, 2)),
            dma((NX, 2, 2)),
            dma((NX, 2, 2)),
            dma((4,)),
            dma((4,)),
        ],
        compiler_params=pltpu.CompilerParams(
            collective_id=0, has_side_effects=True, vmem_limit_bytes=40 * 2**20),
        cost_estimate=pl.CostEstimate(
            flops=2 * ROWS * D * OUT, bytes_accessed=10 * 2**20, transcendentals=5 * ROWS * OUT),
        name="eta_filter",
    )(
        pltpu.with_memory_space_constraint(hidden.T, pltpu.HBM),
        pltpu.with_memory_space_constraint(head_weight.T, pltpu.HBM),
        eta_level.reshape(4, 128),
    )
    return logs - lkm.reshape(ROWS)[:, None], ent.reshape(ROWS)


def solution(mesh):
    return jax.shard_map(
        shards,
        mesh=mesh,
        in_specs=(P("rows", None), P(None, ("vocab", "rows")), P("rows")),
        out_specs=(P("rows", "vocab"), P("rows")),
        check_vma=False,
    )
```

time: 98.3 us -> 68.9 us (0.70); the launches traced: 98.2 us -> 67.8 us
  Pallas kernels: 85.4 us -> 63.8 us
  local copies, waits for them, and re-layouts: 8.15 us -> 1.25 us
  other arithmetic: 4 us -> 2.04 us
    pallas_call x1, Pallas kernels: 85.4 us -> 63.8 us  [shards(): pl.pallas_call(kernel, out_shape=(jax.ShapeDtypeStruct((ROWS, OUT), F32),...]
    unnamed x7 -> x3, local copies, waits for them, and re-layouts: 8.15 us -> 1.25 us
    sub x1, other arithmetic: 4 us -> 2.04 us  [shards(): return (logs - lkm.reshape(ROWS)[:, None], ent.reshape(ROWS))]
where the time goes in v2:
time: 68.9 us; the launch traced here: 67.8 us
  Pallas kernels  63.8 us (93%)
  other arithmetic  2.04 us (3%)
  local copies, waits for them, and re-layouts  1.25 us (2%)
    pallas_call x1, Pallas kernels, shards(): pl.pallas_call(kernel, out_shape=(jax.ShapeDtypeStruct((ROWS, OUT), F32),...  63.8 us
    sub x1, other arithmetic, shards(): return (logs - lkm.reshape(ROWS)[:, None], ent.reshape(ROWS))  2.04 us

profile of v2, /device:TPU:7, one launch (start us, length us, event | category | flops | bytes accessed | tf_op | source)
XLA Modules:
  0.0 67.8 jit_solution(12619081150289665234)
XLA Ops:
  0.6 0.0 copy-start
  0.6 0.7 copy-done
  1.3 63.8 %eta_filter.1 = (f32[512,1664]{1,0:T(8,128)S(1)}, f32[4,128]{1,0:T(4,128)S(1)}, f32[4,128]{1,0:T(4,128)S(1)}) custom-call(bf16[2880,512]{1,0:T(8,128)(2,1)} %bitcast.8, bf16[416,2880]{1,0:T(8,128)(2,1)} %bitcast.9, f32[4,128]{1,0:T(4,128)S(1)} %bitcast.7), custom_call_target="tpu_custom_call" | custom-call | flops 4907335680 | bytes 10485760 | tf_op jit(solution)/shard_map/eta_filter/pallas_call | solution.py:363
  65.1 2.0 %broadcast_subtract_fusion = f32[512,1664]{1,0:T(8,128)} fusion(f32[512,1664]{1,0:T(8,128)S(1)} %get-tuple-element.5, f32[512]{0:T(512)S(1)} %bitcast.5), kind=kLoop, calls=%fused_computation | loop fusion | flops 851968 | bytes 6817792 | tf_op jit(solution)/shard_map/sub | solution.py:416
  67.2 0.6 copy.6
Async XLA Ops:
  0.6 0.7 %copy-start = (f32[512]{0:T(512)S(1)}, f32[512]{0:T(512)}, u32[]{:S(2)}) copy-start(f32[512]{0:T(512)} %param.5) | copy-start | bytes 6148

commit v3 on v2

--- a/solution.py
+++ b/solution.py
@@ -34,9 +34,9 @@
 
 
 def kernel(
-    hid_hbm, w_hbm, eta_ref,
+    hid_hbm, w_hbm, eta_hbm,
     log_ref, lkm_ref, ent_ref,
-    hid, w, codes, stats, got, gstat, keep,
+    hid, w, eta_ref, codes, stats, got, gstat, keep,
     cols, part, zpart, ypart, kept, zkept, ykept,
     load_sem, send_sem, w_sem, x_sem, z_sem, y_sem, code_sem, stat_sem, round_sem, rsend_sem,
 ):
@@ -76,6 +76,7 @@
         for lg in range(2)
     ]
     own.append(pltpu.make_async_copy(w_hbm, w.at[0], load_sem.at[2]))
+    own.append(pltpu.make_async_copy(eta_hbm, eta_ref, load_sem.at[3]))
     for copy in own:
         copy.start()
     part[...] = jnp.zeros_like(part)
@@ -318,21 +319,33 @@
         cols[:, k, :] = (peaks[k] - top) * LOG2E - under
     cols[:, NX, :] = limit
 
-    await_groups(lambda xs, h, lg: got.at[h, lg, pl.ds(pl.multiple_of(COLS * xs, 16), COLS)], code_sem)
-
-    def weigh(group, _):
+    def await_codes(s):
+        cols_from = pl.ds(pl.multiple_of(COLS * xto[s], 16), COLS)
+        for h in ((1 - c,) if s == 0 else (c, 1 - c)):
+            for lg in range(2):
+                ref = got.at[h, lg, cols_from]
+                pltpu.make_async_copy(ref, ref, code_sem.at[xto[s], h, lg]).wait()
+
+    def weigh(group, sources):
         cut = cols[group, NX : NX + 1]
         mass = jnp.zeros((1, 128), F32)
-        for k in range(NX):
-            sent = got[group // 2, group % 2, COLS * k : COLS * (k + 1)].astype(F32)
-            prob = jnp.exp2(jnp.log2(sent) * (1.0 / GAIN) + cols[group, k : k + 1])
+        for s in sources:
+            cols_from = pl.ds(pl.multiple_of(COLS * xto[s], 16), COLS)
+            sent = got[group // 2, group % 2, cols_from].astype(F32)
+            prob = jnp.exp2(jnp.log2(sent) * (1.0 / GAIN) + cols[group, pl.ds(xto[s], 1)])
             weight = jnp.maximum(prob - cut, 0.0)
-            keep[group, COLS * k : COLS * (k + 1)] = weight
+            keep[group, cols_from] = weight
             mass = mass + jnp.sum(weight, axis=0, keepdims=True)
-        kept[pl.ds(group, 1)] = mass
-        return 0
-
-    lax.fori_loop(0, 4, weigh, 0)
+        kept[pl.ds(group, 1)] = kept[pl.ds(group, 1)] + mass
+
+    for sources in ((0, 1, 3), (2,)):
+        for s in sources:
+            await_codes(s)
+
+        def weigh_group(group, _, sources=sources):
+            weigh(group, sources)
+            return 0
+        lax.fori_loop(0, 4, weigh_group, 0)
 
     def finish(group, _):
         least = 0.001 * cols[group, NX : NX + 1]
@@ -355,6 +368,21 @@
     for n, ref in ((0, hid.at[pl.ds(0, 3)]), (2, codes.at[pl.ds(0, 7)]), (3, stats.at[pl.ds(0, 7)])):
         pltpu.make_async_copy(ref, ref, send_sem.at[n]).wait()
     w_out.wait_send()
+
+
+def write_out(log_ref, lkm_ref, ent_ref, out_hbm, ent_out, out, sem):
+    copies = []
+    for group in range(4):
+        rows = slice(128 * group, 128 * group + 128)
+        less = jnp.broadcast_to(lkm_ref[group : group + 1], (128, 128)).T
+        for tile in range(OUT // 128):
+            at_tile = slice(128 * tile, 128 * tile + 128)
+            out[group, :, at_tile] = log_ref[rows, at_tile] - less
+        copies.append(pltpu.make_async_copy(out.at[group], out_hbm.at[rows], sem.at[group]))
+        copies[-1].start()
+    ent_out[...] = ent_ref[...]
+    for copy in copies:
+        copy.wait()
 
 
 def shards(hidden, head_weight, eta_level):
@@ -370,7 +398,7 @@
         in_specs=[
             pl.BlockSpec(memory_space=pltpu.HBM),
             pl.BlockSpec(memory_space=pltpu.HBM),
-            pl.BlockSpec(memory_space=vmem),
+            pl.BlockSpec(memory_space=pltpu.HBM),
         ],
         out_specs=(
             pl.BlockSpec(memory_space=vmem),
@@ -380,6 +408,7 @@
         scratch_shapes=[
             vmem((4, 2, D, 128), BF16),
             vmem((2, COLS, D), BF16),
+            vmem((4, 128), F32),
             vmem((8, 2, COLS, 128), BF16),
             vmem((8, 2, 8, 128), F32),
             vmem((2, 2, OUT, 128), BF16),
@@ -392,7 +421,7 @@
             vmem((8, 128), F32),
             vmem((8, 8, 128), F32),
             vmem((8, 8, 128), F32),
-            dma((3,)),
+            dma((4,)),
             dma((4,)),
             dma((1,)),
             dma((4, 2, 2)),
@@ -411,9 +440,19 @@
     )(
         pltpu.with_memory_space_constraint(hidden.T, pltpu.HBM),
         pltpu.with_memory_space_constraint(head_weight.T, pltpu.HBM),
-        eta_level.reshape(4, 128),
+        pltpu.with_memory_space_constraint(eta_level.reshape(4, 128), pltpu.HBM),
     )
-    return logs - lkm.reshape(ROWS)[:, None], ent.reshape(ROWS)
+    filtered, entropy = pl.pallas_call(
+        write_out,
+        out_shape=(jax.ShapeDtypeStruct((ROWS, OUT), F32), jax.ShapeDtypeStruct((4, 128), F32)),
+        in_specs=[pl.BlockSpec(memory_space=vmem)] * 3,
+        out_specs=(pl.BlockSpec(memory_space=pltpu.HBM), pl.BlockSpec(memory_space=vmem)),
+        scratch_shapes=[vmem((4, 128, OUT), F32), dma((4,))],
+        compiler_params=pltpu.CompilerParams(vmem_limit_bytes=16 * 2**20),
+        cost_estimate=pl.CostEstimate(flops=ROWS * OUT, bytes_accessed=4 * ROWS * OUT, transcendentals=0),
+        name="write_out",
+    )(pltpu.with_memory_space_constraint(logs, vmem), lkm, ent)
+    return filtered, entropy.reshape(ROWS)
 
 
 def solution(mesh):

time: 68.9 us -> 68.6 us (level)
  Pallas kernels: 63.8 us -> 67.1 us
  other arithmetic: 2.04 us -> 0 us
  local copies, waits for them, and re-layouts: 1.25 us -> 0 us
    pallas_call x0 -> x1, Pallas kernels: none -> 2.53 us  [shards(): pl.pallas_call(write_out, out_shape=(jax.ShapeDtypeStruct((ROWS, OUT), F3...]
    sub x1 -> x0, other arithmetic: 2.04 us -> none  [shards(): return (logs - lkm.reshape(ROWS)[:, None], ent.reshape(ROWS))]
    unnamed x3 -> x0, local copies, waits for them, and re-layouts: 1.25 us -> none
    pallas_call x1, Pallas kernels: 63.8 us -> 64.5 us  [shards(): pl.pallas_call(kernel, out_shape=(jax.ShapeDtypeStruct((ROWS, OUT), F32),...]
where the time goes in v3:
time: 68.6 us; the launch traced here: 67.7 us
  Pallas kernels  67.1 us (98%)
    pallas_call x1, Pallas kernels, shards(): pl.pallas_call(kernel, out_shape=(jax.ShapeDtypeStruct((ROWS, OUT), F32),...  64.5 us
    pallas_call x1, Pallas kernels, shards(): pl.pallas_call(write_out, out_shape=(jax.ShapeDtypeStruct((ROWS, OUT), F3...  2.53 us

profile of v3, /device:TPU:7, one launch (start us, length us, event | category | flops | bytes accessed | tf_op | source)
XLA Modules:
  0.0 67.7 jit_solution(861581318203671185)
XLA Ops:
  0.6 64.5 %eta_filter.1 = (f32[512,1664]{1,0:T(8,128)S(1)}, f32[4,128]{1,0:T(4,128)S(1)}, f32[4,128]{1,0:T(4,128)S(1)}) custom-call(bf16[2880,512]{1,0:T(8,128)(2,1)} %bitcast.4, bf16[416,2880]{1,0:T(8,128)(2,1)} %bitcast.5, f32[4,128]{1,0:T(4,128)} %bitcast.6), custom_call_target="tpu_custom_call" | custom-call | flops 4907335680 | bytes 10485760 | tf_op jit(solution)/shard_map/eta_filter/pallas_call | solution.py:391
  65.2 2.5 %write_out.1 = (f32[512,1664]{1,0:T(8,128)}, f32[4,128]{1,0:T(4,128)}) custom-call(f32[512,1664]{1,0:T(8,128)S(1)} %get-tuple-element.7.log_ref, f32[4,128]{1,0:T(4,128)S(1)} %get-tuple-element.8.lkm_ref, f32[4,128]{1,0:T(4,128)S(1)} %get-tuple-element.9.ent_ref), custom_call_target="tpu_custom_call" | custom-call | flops 851968 | bytes 3407872 | tf_op jit(solution)/shard_map/write_out/pallas_call | solution.py:445

commit v4 on v3

--- a/solution.py
+++ b/solution.py
@@ -294,30 +294,6 @@
     def swap_end(slots, n):
         seven = slots.at[pl.ds(0, 7)]
         pltpu.make_async_copy(seven, seven, round_sem.at[n]).wait()
-        pltpu.make_async_copy(seven, seven, rsend_sem.at[n]).wait()
-
-    peaks = [gstat[k, :, 0, :] for k in range(NX)]
-    top, total, moment = combined(
-        peaks, [gstat[k, :, 1, :] for k in range(NX)], [gstat[k, :, 2, :] for k in range(NX)])
-    yc = y * 2 + c
-    for slots, place_at, peer_set, n in ((zpart, z, zpeers, 0), (ypart, yc, ypeers, 1)):
-        part[0:4] = top
-        part[4:8] = total
-        part[8:12] = moment
-        swap_start(part, slots, place_at, peer_set, n)
-        swap_end(slots, n)
-        top, total, moment = combined(
-            [slots[k, 0:4] for k in range(8)], [slots[k, 4:8] for k in range(8)],
-            [slots[k, 8:12] for k in range(8)])
-
-    eta = eta_ref[...]
-    entropy = jnp.log(total) - moment / total * LN2
-    limit = jnp.minimum(eta, jnp.sqrt(eta) * jnp.exp(-entropy))
-    ent_ref[...] = entropy
-    under = jnp.log2(total) + BIAS / GAIN
-    for k in range(NX):
-        cols[:, k, :] = (peaks[k] - top) * LOG2E - under
-    cols[:, NX, :] = limit
 
     def await_codes(s):
         cols_from = pl.ds(pl.multiple_of(COLS * xto[s], 16), COLS)
@@ -326,21 +302,55 @@
                 ref = got.at[h, lg, cols_from]
                 pltpu.make_async_copy(ref, ref, code_sem.at[xto[s], h, lg]).wait()
 
+    def decode(sources):
+        for s in sources:
+            await_codes(s)
+
+        def one(group, _):
+            for s in sources:
+                cols_from = pl.ds(pl.multiple_of(COLS * xto[s], 16), COLS)
+                sent = got[group // 2, group % 2, cols_from].astype(F32)
+                keep[group, cols_from] = jnp.exp2((jnp.log2(sent) - BIAS) * (1.0 / GAIN))
+            return 0
+        lax.fori_loop(0, 4, one, 0)
+
+    peaks = [gstat[k, :, 0, :] for k in range(NX)]
+    top, total, moment = combined(
+        peaks, [gstat[k, :, 1, :] for k in range(NX)], [gstat[k, :, 2, :] for k in range(NX)])
+    yc = y * 2 + c
+    for slots, place_at, peer_set, n in ((zpart, z, zpeers, 0), (ypart, yc, ypeers, 1)):
+        part[n, 0] = top
+        part[n, 1] = total
+        part[n, 2] = moment
+        swap_start(part.at[n], slots, place_at, peer_set, n)
+        decode(((0, 1), (3,))[n])
+        swap_end(slots, n)
+        top, total, moment = combined(
+            *([slots[k, n] for k in range(8)] for n in range(3)))
+
+    eta = eta_ref[...]
+    entropy = jnp.log(total) - moment / total * LN2
+    limit = jnp.minimum(eta, jnp.sqrt(eta) * jnp.exp(-entropy))
+    ent_ref[...] = entropy
+    under = jnp.log2(total)
+    for k in range(NX):
+        cols[:, k, :] = jnp.exp2((peaks[k] - top) * LOG2E - under)
+    cols[:, NX, :] = limit
+
     def weigh(group, sources):
         cut = cols[group, NX : NX + 1]
         mass = jnp.zeros((1, 128), F32)
         for s in sources:
             cols_from = pl.ds(pl.multiple_of(COLS * xto[s], 16), COLS)
-            sent = got[group // 2, group % 2, cols_from].astype(F32)
-            prob = jnp.exp2(jnp.log2(sent) * (1.0 / GAIN) + cols[group, pl.ds(xto[s], 1)])
+            prob = keep[group, cols_from] * cols[group, pl.ds(xto[s], 1)]
             weight = jnp.maximum(prob - cut, 0.0)
             keep[group, cols_from] = weight
             mass = mass + jnp.sum(weight, axis=0, keepdims=True)
-        kept[pl.ds(group, 1)] = kept[pl.ds(group, 1)] + mass
+        kept[0, pl.ds(group, 1)] = kept[0, pl.ds(group, 1)] + mass
 
     for sources in ((0, 1, 3), (2,)):
-        for s in sources:
-            await_codes(s)
+        if sources == (2,):
+            decode(sources)
 
         def weigh_group(group, _, sources=sources):
             weigh(group, sources)
@@ -356,17 +366,21 @@
         return 0
 
     for slots, place_at, peer_set, n in ((zkept, z, zpeers, 2), (ykept, yc, ypeers, 3)):
-        swap_start(kept, slots, place_at, peer_set, n)
+        swap_start(kept.at[n - 2], slots, place_at, peer_set, n)
         lax.fori_loop(2 * n - 4, 2 * n - 2, finish, 0)
         swap_end(slots, n)
         mass = slots[0]
         for k in range(1, 8):
             mass = mass + slots[k]
-        kept[...] = mass
-    lkm_ref[...] = jnp.log(kept[0:4])
+        if n == 2:
+            kept[1] = mass
+    lkm_ref[...] = jnp.log(mass)
 
     for n, ref in ((0, hid.at[pl.ds(0, 3)]), (2, codes.at[pl.ds(0, 7)]), (3, stats.at[pl.ds(0, 7)])):
         pltpu.make_async_copy(ref, ref, send_sem.at[n]).wait()
+    for n, slots in enumerate((zpart, ypart, zkept, ykept)):
+        seven = slots.at[pl.ds(0, 7)]
+        pltpu.make_async_copy(seven, seven, rsend_sem.at[n]).wait()
     w_out.wait_send()
 
 
@@ -415,12 +429,12 @@
             vmem((NX, 4, 8, 128), F32),
             vmem((4, OUT, 128), F32),
             vmem((4, 8, 128), F32),
-            vmem((16, 128), F32),
-            vmem((8, 16, 128), F32),
-            vmem((8, 16, 128), F32),
-            vmem((8, 128), F32),
-            vmem((8, 8, 128), F32),
-            vmem((8, 8, 128), F32),
+            vmem((2, 3, 4, 128), F32),
+            vmem((8, 3, 4, 128), F32),
+            vmem((8, 3, 4, 128), F32),
+            vmem((2, 4, 128), F32),
+            vmem((8, 4, 128), F32),
+            vmem((8, 4, 128), F32),
             dma((4,)),
             dma((4,)),
             dma((1,)),

time: 68.6 us -> 71.9 us (1.048); the launches traced: 67.7 us -> 71.8 us
  Pallas kernels: 67.1 us -> 71.2 us
    pallas_call x1, Pallas kernels: 64.5 us -> 68.7 us  [shards(): pl.pallas_call(kernel, out_shape=(jax.ShapeDtypeStruct((ROWS, OUT), F32),...]
where the time goes in v4:
time: 71.9 us; the launch traced here: 71.8 us
  Pallas kernels  71.2 us (99%)
    pallas_call x1, Pallas kernels, shards(): pl.pallas_call(kernel, out_shape=(jax.ShapeDtypeStruct((ROWS, OUT), F32),...  68.7 us
    pallas_call x1, Pallas kernels, shards(): pl.pallas_call(write_out, out_shape=(jax.ShapeDtypeStruct((ROWS, OUT), F3...  2.53 us

profile of v4, /device:TPU:7, one launch (start us, length us, event | category | flops | bytes accessed | tf_op | source)
XLA Modules:
  0.0 71.8 jit_solution(12625156838262948828)
XLA Ops:
  0.6 68.7 %eta_filter.1 = (f32[512,1664]{1,0:T(8,128)S(1)}, f32[4,128]{1,0:T(4,128)S(1)}, f32[4,128]{1,0:T(4,128)S(1)}) custom-call(bf16[2880,512]{1,0:T(8,128)(2,1)} %bitcast.4, bf16[416,2880]{1,0:T(8,128)(2,1)} %bitcast.5, f32[4,128]{1,0:T(4,128)} %bitcast.6), custom_call_target="tpu_custom_call" | custom-call | flops 4907335680 | bytes 10485760 | tf_op jit(solution)/shard_map/eta_filter/pallas_call | solution.py:405
  69.3 2.5 %write_out.1 = (f32[512,1664]{1,0:T(8,128)}, f32[4,128]{1,0:T(4,128)}) custom-call(f32[512,1664]{1,0:T(8,128)S(1)} %get-tuple-element.7.log_ref, f32[4,128]{1,0:T(4,128)S(1)} %get-tuple-element.8.lkm_ref, f32[4,128]{1,0:T(4,128)S(1)} %get-tuple-element.9.ent_ref), custom_call_target="tpu_custom_call" | custom-call | flops 851968 | bytes 3407872 | tf_op jit(solution)/shard_map/write_out/pallas_call | solution.py:459

commit v5 on v4

--- a/solution.py
+++ b/solution.py
@@ -295,25 +295,6 @@
         seven = slots.at[pl.ds(0, 7)]
         pltpu.make_async_copy(seven, seven, round_sem.at[n]).wait()
 
-    def await_codes(s):
-        cols_from = pl.ds(pl.multiple_of(COLS * xto[s], 16), COLS)
-        for h in ((1 - c,) if s == 0 else (c, 1 - c)):
-            for lg in range(2):
-                ref = got.at[h, lg, cols_from]
-                pltpu.make_async_copy(ref, ref, code_sem.at[xto[s], h, lg]).wait()
-
-    def decode(sources):
-        for s in sources:
-            await_codes(s)
-
-        def one(group, _):
-            for s in sources:
-                cols_from = pl.ds(pl.multiple_of(COLS * xto[s], 16), COLS)
-                sent = got[group // 2, group % 2, cols_from].astype(F32)
-                keep[group, cols_from] = jnp.exp2((jnp.log2(sent) - BIAS) * (1.0 / GAIN))
-            return 0
-        lax.fori_loop(0, 4, one, 0)
-
     peaks = [gstat[k, :, 0, :] for k in range(NX)]
     top, total, moment = combined(
         peaks, [gstat[k, :, 1, :] for k in range(NX)], [gstat[k, :, 2, :] for k in range(NX)])
@@ -323,7 +304,6 @@
         part[n, 1] = total
         part[n, 2] = moment
         swap_start(part.at[n], slots, place_at, peer_set, n)
-        decode(((0, 1), (3,))[n])
         swap_end(slots, n)
         top, total, moment = combined(
             *([slots[k, n] for k in range(8)] for n in range(3)))
@@ -332,25 +312,33 @@
     entropy = jnp.log(total) - moment / total * LN2
     limit = jnp.minimum(eta, jnp.sqrt(eta) * jnp.exp(-entropy))
     ent_ref[...] = entropy
-    under = jnp.log2(total)
+    under = jnp.log2(total) + BIAS / GAIN
     for k in range(NX):
-        cols[:, k, :] = jnp.exp2((peaks[k] - top) * LOG2E - under)
+        cols[:, k, :] = (peaks[k] - top) * LOG2E - under
     cols[:, NX, :] = limit
+
+    def await_codes(s):
+        cols_from = pl.ds(pl.multiple_of(COLS * xto[s], 16), COLS)
+        for h in ((1 - c,) if s == 0 else (c, 1 - c)):
+            for lg in range(2):
+                ref = got.at[h, lg, cols_from]
+                pltpu.make_async_copy(ref, ref, code_sem.at[xto[s], h, lg]).wait()
 
     def weigh(group, sources):
         cut = cols[group, NX : NX + 1]
         mass = jnp.zeros((1, 128), F32)
         for s in sources:
             cols_from = pl.ds(pl.multiple_of(COLS * xto[s], 16), COLS)
-            prob = keep[group, cols_from] * cols[group, pl.ds(xto[s], 1)]
+            sent = got[group // 2, group % 2, cols_from].astype(F32)
+            prob = jnp.exp2(jnp.log2(sent) * (1.0 / GAIN) + cols[group, pl.ds(xto[s], 1)])
             weight = jnp.maximum(prob - cut, 0.0)
             keep[group, cols_from] = weight
             mass = mass + jnp.sum(weight, axis=0, keepdims=True)
         kept[0, pl.ds(group, 1)] = kept[0, pl.ds(group, 1)] + mass
 
     for sources in ((0, 1, 3), (2,)):
-        if sources == (2,):
-            decode(sources)
+        for s in sources:
+            await_codes(s)
 
         def weigh_group(group, _, sources=sources):
             weigh(group, sources)

time: 71.9 us -> 68.5 us (0.953); the launches traced: 71.8 us -> 67.6 us
  Pallas kernels: 71.2 us -> 67 us
    pallas_call x1, Pallas kernels: 68.7 us -> 64.5 us  [shards(): pl.pallas_call(kernel, out_shape=(jax.ShapeDtypeStruct((ROWS, OUT), F32),...]
where the time goes in v5:
time: 68.5 us; the launch traced here: 67.6 us
  Pallas kernels  67 us (98%)
    pallas_call x1, Pallas kernels, shards(): pl.pallas_call(kernel, out_shape=(jax.ShapeDtypeStruct((ROWS, OUT), F32),...  64.5 us
    pallas_call x1, Pallas kernels, shards(): pl.pallas_call(write_out, out_shape=(jax.ShapeDtypeStruct((ROWS, OUT), F3...  2.53 us

profile of v5, /device:TPU:7, one launch (start us, length us, event | category | flops | bytes accessed | tf_op | source)
XLA Modules:
  0.0 67.6 jit_solution(5930161133088596071)
XLA Ops:
  0.6 64.5 %eta_filter.1 = (f32[512,1664]{1,0:T(8,128)S(1)}, f32[4,128]{1,0:T(4,128)S(1)}, f32[4,128]{1,0:T(4,128)S(1)}) custom-call(bf16[2880,512]{1,0:T(8,128)(2,1)} %bitcast.4, bf16[416,2880]{1,0:T(8,128)(2,1)} %bitcast.5, f32[4,128]{1,0:T(4,128)} %bitcast.6), custom_call_target="tpu_custom_call" | custom-call | flops 4907335680 | bytes 10485760 | tf_op jit(solution)/shard_map/eta_filter/pallas_call | solution.py:393
  65.1 2.5 %write_out.1 = (f32[512,1664]{1,0:T(8,128)}, f32[4,128]{1,0:T(4,128)}) custom-call(f32[512,1664]{1,0:T(8,128)S(1)} %get-tuple-element.7.log_ref, f32[4,128]{1,0:T(4,128)S(1)} %get-tuple-element.8.lkm_ref, f32[4,128]{1,0:T(4,128)S(1)} %get-tuple-element.9.ent_ref), custom_call_target="tpu_custom_call" | custom-call | flops 851968 | bytes 3407872 | tf_op jit(solution)/shard_map/write_out/pallas_call | solution.py:447

commit v6 on v5

--- a/solution.py
+++ b/solution.py
@@ -372,8 +372,9 @@
     w_out.wait_send()
 
 
-def write_out(log_ref, lkm_ref, ent_ref, out_hbm, ent_out, out, sem):
-    copies = []
+def write_out(log_ref, lkm_ref, ent_ref, out_hbm, ent_hbm, out, sem):
+    copies = [pltpu.make_async_copy(ent_ref, ent_hbm, sem.at[4])]
+    copies[0].start()
     for group in range(4):
         rows = slice(128 * group, 128 * group + 128)
         less = jnp.broadcast_to(lkm_ref[group : group + 1], (128, 128)).T
@@ -382,7 +383,6 @@
             out[group, :, at_tile] = log_ref[rows, at_tile] - less
         copies.append(pltpu.make_async_copy(out.at[group], out_hbm.at[rows], sem.at[group]))
         copies[-1].start()
-    ent_out[...] = ent_ref[...]
     for copy in copies:
         copy.wait()
 
@@ -448,8 +448,8 @@
         write_out,
         out_shape=(jax.ShapeDtypeStruct((ROWS, OUT), F32), jax.ShapeDtypeStruct((4, 128), F32)),
         in_specs=[pl.BlockSpec(memory_space=vmem)] * 3,
-        out_specs=(pl.BlockSpec(memory_space=pltpu.HBM), pl.BlockSpec(memory_space=vmem)),
-        scratch_shapes=[vmem((4, 128, OUT), F32), dma((4,))],
+        out_specs=(pl.BlockSpec(memory_space=pltpu.HBM), pl.BlockSpec(memory_space=pltpu.HBM)),
+        scratch_shapes=[vmem((4, 128, OUT), F32), dma((5,))],
         compiler_params=pltpu.CompilerParams(vmem_limit_bytes=16 * 2**20),
         cost_estimate=pl.CostEstimate(flops=ROWS * OUT, bytes_accessed=4 * ROWS * OUT, transcendentals=0),
         name="write_out",

time: 68.5 us -> 67.9 us (level)
  no operation moved by 1% of the time
where the time goes in v6:
time: 67.9 us; the launch traced here: 67.1 us
  Pallas kernels  66.4 us (98%)
    pallas_call x1, Pallas kernels, shards(): pl.pallas_call(kernel, out_shape=(jax.ShapeDtypeStruct((ROWS, OUT), F32),...  64.5 us
    pallas_call x1, Pallas kernels, shards(): pl.pallas_call(write_out, out_shape=(jax.ShapeDtypeStruct((ROWS, OUT), F3...  1.95 us

profile of v6, /device:TPU:7, one launch (start us, length us, event | category | flops | bytes accessed | tf_op | source)
XLA Modules:
  0.0 67.1 jit_solution(10475241948533974087)
XLA Ops:
  0.6 64.5 %eta_filter.1 = (f32[512,1664]{1,0:T(8,128)S(1)}, f32[4,128]{1,0:T(4,128)S(1)}, f32[4,128]{1,0:T(4,128)S(1)}) custom-call(bf16[2880,512]{1,0:T(8,128)(2,1)} %bitcast.4, bf16[416,2880]{1,0:T(8,128)(2,1)} %bitcast.5, f32[4,128]{1,0:T(4,128)} %bitcast.6), custom_call_target="tpu_custom_call" | custom-call | flops 4907335680 | bytes 10485760 | tf_op jit(solution)/shard_map/eta_filter/pallas_call | solution.py:393
  65.1 2.0 %write_out.1 = (f32[512,1664]{1,0:T(8,128)}, f32[4,128]{1,0:T(4,128)}) custom-call(f32[512,1664]{1,0:T(8,128)S(1)} %get-tuple-element.7.log_ref, f32[4,128]{1,0:T(4,128)S(1)} %get-tuple-element.8.lkm_ref, f32[4,128]{1,0:T(4,128)S(1)} %get-tuple-element.9.ent_ref), custom_call_target="tpu_custom_call" | custom-call | flops 851968 | bytes 3407872 | tf_op jit(solution)/shard_map/write_out/pallas_call | solution.py:447
